TPU v7x, 512 devices: a whole 4x8x8 slice. The times are simulated.
512 devices in a mesh: grp: 8 (over y_hi, core), seq: 64 (over z, x, y_lo).
Axes of the slice: x: 4, y: 8 (y_hi: 4, y_lo: 2; y = y_hi * 2 + y_lo), z: 8, core: 2. Of those that a mesh axis runs over, the one named last changes fastest.
Arguments:
- queries: bfloat16 [64, 24, 256, 128], P('grp', None, 'seq'), may hold values from -8 to 8
- keys: bfloat16 [64, 24, 256, 128], P('grp', None, 'seq'), may hold values from -6 to 6
- values: bfloat16 [64, 24, 256, 128], P('grp', None, 'seq'), may hold values from -6 to 6
- context: bfloat16 [256, 4096], P(None, 'grp'), may hold values from -6 to 6
- residual: bfloat16 [256, 4096], P('grp', 'seq'), may hold values from -6 to 6
- codes: int32 [4096, 4096], P('grp', 'seq'), may hold values from -127 to 127
- scales: float32 [32, 4096], P('grp', 'seq'), may hold values from 0.0001 to 0.0004
- gain: float32 [4096], P('seq'), may hold values from 0.5 to 1.5
- kv_weight: bfloat16 [4096, 6144], P(None, 'seq'), may hold values from -1 to 1
- lengths: int32 [4], replicated, may hold values from 1 to 64, 160 in all
Outputs:
- attended: bfloat16 [64, 24, 256, 128], P('grp', None, 'seq')
Inputs may be any that keep to these rules, and one draw needn't show every extreme that they name: The lengths sum to 160 and one of them is exactly 64.
All inputs are finite; a program needn't handle non-finite values.
Results may differ from a plain program's by a relative error of at most 0.0071.
Values may be sent and summed in bfloat16 or wider, within the bound.
A program may use at most 64 MiB of HBM per device.

v0:
```python
import math

import jax
import jax.numpy as jnp
from jax import lax
from jax.sharding import PartitionSpec as P

D_TEXT = 4096
QGROUP = 128
PROMPTS = 4
TLEN = 64


def softmax_rows(scores):
    top = jnp.max(scores, axis=-1, keepdims=True)
    weights = jnp.exp(scores - top)
    return weights / jnp.sum(weights, axis=-1, keepdims=True)


def local(queries, keys, values, context, residual, codes, scales, gain, kv_weight, lengths):
    weight = (codes.astype(jnp.float32) * jnp.repeat(scales, QGROUP, axis=0)).astype(jnp.bfloat16)
    block = context
    hidden = residual.astype(jnp.float32) + lax.psum_scatter(
        jnp.dot(block, weight, preferred_element_type=jnp.float32),
        "grp",
        scatter_dimension=0,
        tiled=True,
    )
    squares = lax.psum(jnp.sum(hidden * hidden, axis=1), "seq")
    text = (hidden * lax.rsqrt(squares[:, None] / D_TEXT + 1e-06) * gain).astype(jnp.bfloat16)
    all_text = lax.all_gather(text, "grp", axis=0, tiled=True)
    kv_part = jnp.dot(
        lax.all_gather(all_text, "seq", axis=1, tiled=True),
        kv_weight,
        preferred_element_type=jnp.float32,
    ).astype(jnp.bfloat16)
    text_kv = lax.all_gather(kv_part, "seq", axis=1, tiled=True)
    videos, heads, tokens, head_dim = queries.shape
    width = heads * head_dim
    prompt_keys = text_kv[:, :width].reshape(PROMPTS, TLEN, heads, head_dim)
    prompt_values = text_kv[:, width:].reshape(PROMPTS, TLEN, heads, head_dim)
    factor = 1.0 / math.sqrt(head_dim)
    parts = lax.axis_size("seq")

    def split_pairs(block):
        return block.reshape(parts, videos * heads // parts, tokens, head_dim)

    def self_pair(pair):
        query_rows, key_rows, value_rows = pair
        scores = jnp.dot(query_rows, key_rows.T, preferred_element_type=jnp.float32) * factor
        probs = softmax_rows(scores).astype(jnp.bfloat16)
        return jnp.dot(probs, value_rows, preferred_element_type=jnp.float32).astype(jnp.bfloat16)

    query_rows = lax.all_to_all(
        split_pairs(queries), "seq", split_axis=0, concat_axis=2, tiled=True
    )
    key_rows = lax.all_to_all(split_pairs(keys), "seq", split_axis=0, concat_axis=2, tiled=True)
    value_rows = lax.all_to_all(split_pairs(values), "seq", split_axis=0, concat_axis=2, tiled=True)
    head_out = lax.map(self_pair, (query_rows[0], key_rows[0], value_rows[0]))[None]
    self_out = lax.all_to_all(head_out, "seq", split_axis=2, concat_axis=0, tiled=True).reshape(
        queries.shape
    )
    row_place = jnp.arange(TLEN, dtype=jnp.int32)
    live_rows = row_place[None, :] < lengths[:, None]
    grouped = queries.reshape(videos // PROMPTS, PROMPTS, heads, tokens, head_dim)
    scores = (
        jnp.einsum("gphtd,prhd->gphtr", grouped, prompt_keys, preferred_element_type=jnp.float32)
        * factor
    )
    scores = jnp.where(live_rows[None, :, None, None, :], scores, -1e30)
    cross_probs = softmax_rows(scores).astype(jnp.bfloat16)
    cross_out = jnp.einsum(
        "gphtr,prhd->gphtd", cross_probs, prompt_values, preferred_element_type=jnp.float32
    )
    cross_out = cross_out.reshape(queries.shape)
    return (self_out.astype(jnp.float32) + cross_out).astype(jnp.bfloat16)


def solution(mesh):
    placed = (
        P("grp", None, "seq", None),
        P("grp", None, "seq", None),
        P("grp", None, "seq", None),
        P(None, "grp"),
        P("grp", "seq"),
        P("grp", "seq"),
        P("grp", "seq"),
        P("seq"),
        P(None, "seq"),
        P(),
    )
    return jax.shard_map(
        local, mesh=mesh, in_specs=placed, out_specs=P("grp", None, "seq", None), check_vma=False
    )
```

profile of v0, /device:TPU:2, one launch (start us, length us, event | category | flops | bytes accessed | tf_op | source)
XLA Modules:
  0.0 860.7 jit_solution(9965713515917302604)
XLA Ops:
  6.5 0.9 copy.93
  7.5 1.2 convolution_bitcast_fusion
  8.8 0.8 copy.113
  9.6 44.5 %reduce-scatter.4.cloned.1.call-done = f32[32,64]{1,0:T(8,128)} async-done(((f32[256,64]{1,0:T(8,128)}), f32[32,64]{1,0:T(8,128)}) %reduce-scatter.4.cloned.1.call-update) | async-done | bytes 8208 | tf_op jit(solution)/shard_map/reduce_scatter | solution.py:23
  54.1 0.8 multiply_reduce_fusion
  54.9 154.9 %psum.7 = f32[32]{0:T(128)S(1)} all-reduce(f32[32]{0:T(128)S(1)} %multiply_reduce_fusion), channel_id=1, replica_groups=mesh['grp'=8,'seq'=64] {'seq'}, use_global_device_ids=true, to_apply=%region_6.7 | all-reduce | flops 32 | bytes 256 | tf_op jit(solution)/shard_map/psum | solution.py:29
  209.8 0.8 multiply_convert_fusion
  210.7 14.5 %all_gather.9 = bf16[256,64]{1,0:T(8,128)(2,1)S(1)} all-gather(bf16[32,64]{1,0:T(8,128)(2,1)S(1)} %multiply_convert_fusion), channel_id=1, replica_groups=mesh['grp'=8,'seq'=64] {'grp'}, dimensions={0}, use_global_device_ids=true | all-gather | bytes 36864 | tf_op jit(solution)/shard_map/all_gather | solution.py:31
  225.2 0.7 copy.95
  226.0 300.9 %all-gather.3.cloned.1.call-done = bf16[256,4096]{0,1:T(8,128)(2,1)} async-done(((bf16[256,64]{0,1:T(8,128)(2,1)}), bf16[256,4096]{0,1:T(8,128)(2,1)}) %all-gather.3.cloned.1.call-update) | async-done | bytes 2097168 | tf_op jit(solution)/shard_map/all_gather | solution.py:33
  526.9 2.7 convolution_convert_fusion.1
  529.6 17.3 %all_to_all.54 = bf16[64,3,4,128]{3,2,1,0:T(4,128)(2,1)S(1)} all-to-all(bf16[64,3,4,128]{3,2,1,0:T(4,128)(2,1)S(1)} %bitcast.87), channel_id=1, replica_groups=mesh['grp'=8,'seq'=64] {'seq'}, dimensions={0} | all-to-all | bytes 393216 | tf_op jit(solution)/shard_map/all_to_all | solution.py:57
  546.9 18.4 %all_to_all.55 = bf16[64,3,4,128]{3,2,1,0:T(4,128)(2,1)S(1)} all-to-all(bf16[64,3,4,128]{3,2,1,0:T(4,128)(2,1)S(1)} %bitcast.88), channel_id=1, replica_groups=mesh['grp'=8,'seq'=64] {'seq'}, dimensions={0} | all-to-all | bytes 393216 | tf_op jit(solution)/shard_map/all_to_all | solution.py:58
  565.4 5.4 all-to-all-start
  571.0 10.3 %all-to-all-done = bf16[64,3,4,128]{3,2,1,0:T(4,128)(2,1)S(1)} async-done(((bf16[64,3,4,128]{3,2,1,0:T(4,128)(2,1)}), bf16[64,3,4,128]{3,2,1,0:T(4,128)(2,1)S(1)}, u32[]{:S(2)}, u32[]{:S(2)}) %all-to-all-start) | async-done | bytes 196640 | tf_op jit(solution)/shard_map/all_to_all | solution.py:54
  581.4 1.7 while.10
  581.4 0.2 fusion.52
  581.7 0.3 fusion.54
  581.9 0.2 fusion.52
  582.2 0.3 fusion.54
  582.5 0.2 fusion.52
  582.8 0.3 fusion.54
  583.1 0.9 copy.140
  584.0 5.4 all-to-all-start.3
  589.5 11.3 %all-to-all-done.3 = bf16[1,3,256,128]{3,1,0,2:T(4,128)(2,1)S(1)} async-done(((bf16[1,3,256,128]{3,1,0,2:T(4,128)(2,1)}), bf16[1,3,256,128]{3,1,0,2:T(4,128)(2,1)S(1)}, u32[]{:S(2)}, u32[]{:S(2)}) %all-to-all-start.3) | async-done | bytes 196640 | tf_op jit(solution)/shard_map/all_to_all | solution.py:60
  600.9 233.8 %all-gather.5.cloned.1.call-done = bf16[256,6144]{0,1:T(8,128)(2,1)} async-done(((bf16[256,96]{0,1:T(8,128)(2,1)}), bf16[256,6144]{0,1:T(8,128)(2,1)}) %all-gather.5.cloned.1.call-update) | async-done | bytes 3145744 | tf_op jit(solution)/shard_map/all_gather | solution.py:37
  834.7 3.2 fusion.38
  837.9 5.8 reshape.73
  843.7 2.8 reshape.72
  846.5 3.0 fusion.39
  849.6 3.7 fusion.20
  853.3 0.8 fusion.32
  (26 shorter events, 1.0 us)
Async XLA Ops:
  6.5 520.4 %copy-start = (bf16[4096,96]{0,1:T(8,128)(2,1)S(1)}, bf16[4096,96]{0,1:T(8,128)(2,1)}, u32[]{:S(2)}) copy-start(bf16[4096,96]{0,1:T(8,128)(2,1)} %param.20) | copy-start | bytes 2359300
  6.5 523.1 %copy-start.1 = (bf16[8,24,4,128]{3,2,1,0:T(4,128)(2,1)S(1)}, bf16[8,24,4,128]{3,2,1,0:T(4,128)(2,1)}, u32[]{:S(2)}) copy-start(bf16[8,24,4,128]{3,2,1,0:T(4,128)(2,1)} %param.13) | copy-start | bytes 589828
  6.5 540.4 %copy-start.2 = (bf16[8,24,4,128]{3,2,1,0:T(4,128)(2,1)S(1)}, bf16[8,24,4,128]{3,2,1,0:T(4,128)(2,1)}, u32[]{:S(2)}) copy-start(bf16[8,24,4,128]{3,2,1,0:T(4,128)(2,1)} %param.14) | copy-start | bytes 589828
  6.5 47.5 %reduce-scatter.4.cloned.1.call-start = ((), (), s32[]{:S(2)}) async-start(), calls=%async_computation.7 | async-start | bytes 147456 | tf_op jit(solution)/shard_map/reduce_scatter | solution.py:23
  9.6 517.3 %all-gather.3.cloned.1.call-start = ((), (), s32[]{:S(2)}) async-start(), calls=%async_computation.5 | async-start | bytes 2129920 | tf_op jit(solution)/shard_map/all_gather | solution.py:33
  225.9 608.8 %all-gather.5.cloned.1.call-start = ((), (), s32[]{:S(2)}) async-start(), calls=%async_computation.6 | async-start | bytes 3194880 | tf_op jit(solution)/shard_map/all_gather | solution.py:37
  565.4 15.9 %all-to-all-start = ((bf16[64,3,4,128]{3,2,1,0:T(4,128)(2,1)}), bf16[64,3,4,128]{3,2,1,0:T(4,128)(2,1)S(1)}, u32[]{:S(2)}, u32[]{:S(2)}) async-start(bf16[64,3,4,128]{3,2,1,0:T(4,128)(2,1)} %bitcast.4), calls=%async_computation | async-start | bytes 393216 | tf_op jit(solution)/shard_map/all_to_all | solution.py:54
  581.3 8.1 copy-start.3
  584.0 16.8 %all-to-all-start.3 = ((bf16[1,3,256,128]{3,1,0,2:T(4,128)(2,1)}), bf16[1,3,256,128]{3,1,0,2:T(4,128)(2,1)S(1)}, u32[]{:S(2)}, u32[]{:S(2)}) async-start(bf16[1,3,256,128]{3,1,0,2:T(4,128)(2,1)} %bitcast.67), calls=%async_computation.3 | async-start | bytes 524288 | tf_op jit(solution)/shard_map/all_to_all | solution.py:60
Sparse Core Ops, SparseCore 0:
  10.1 43.8 reduce-scatter.3
  226.0 300.7 all-gather.2
  529.7 304.9 all-gather.4
where the time goes:
time: 861 us
  waiting for transfers between devices  601 us (70%)
  blocking collectives  205 us (24%)
  local copies, waits for them, and re-layouts  15.6 us (2%)
  between operations  13.2 us (2%)
  matrix products  12 us (1%)
  starting transfers between devices  10.9 us (1%)
    all_gather x1, waiting for transfers between devices, local(): lax.all_gather(all_text, 'seq', axis=1, tiled=True)  301 us
    all_gather x1, waiting for transfers between devices, local(): text_kv = lax.all_gather(kv_part, 'seq', axis=1, tiled=True)  234 us
    psum x1, blocking collectives, local(): squares = lax.psum(jnp.sum(hidden * hidden, axis=1), 'seq')  155 us
    reduce_scatter x1, waiting for transfers between devices, local(): lax.psum_scatter(jnp.dot(block, weight, preferred_element_type=jnp.float3...  44.5 us
    all_to_all x1, blocking collectives, local(): lax.all_to_all(split_pairs(values), 'seq', split_axis=0, concat_axis=2, t...  18.4 us
    all_to_all x1, blocking collectives, local(): lax.all_to_all(split_pairs(keys), 'seq', split_axis=0, concat_axis=2, til...  17.3 us
  transfers between devices with their start and end apart: 5, of which 5 were waited for; matrix products, arithmetic and copies ran while one was open for 0% of the time, Pallas kernels for 0%

commit v1 on v0

v1 whole, which is shorter than its diff:
```python
import math

import jax
import jax.numpy as jnp
from jax import lax
from jax.experimental import pallas as pl
from jax.experimental.pallas import tpu as pltpu
from jax.sharding import PartitionSpec as P

MESH = pl.DeviceIdType.MESH
BF16 = jnp.bfloat16
F32 = jnp.float32
FACTOR = 1.0 / math.sqrt(128)
D_TEXT = 4096


def dot_t(a, b):
    return lax.dot_general(a, b, (((1,), (1,)), ((), ())), preferred_element_type=F32)


def partner(me, i):
    z, x, y = me // 8, (me // 2) % 4, me % 2
    dz, dx, dy = (i * 3) % 8, (i // 8) % 4, (i // 32 + i) % 2
    return ((z + dz) % 8) * 8 + ((x + dx) % 4) * 2 + (y + dy) % 2


def block_of(p):
    z, x, y = p // 8, (p // 2) % 4, p % 2
    t = (z + 6) % 8
    return ((t // 4) * 4 + (x % 2) * 2 + y) * 8 + (t % 4) * 2 + x // 2


def wait_bytes(ref, sem):
    pltpu.make_async_copy(ref, ref, sem).wait()


def softmax_rows(scores):
    top = jnp.max(scores, axis=-1, keepdims=True)
    weights = jnp.exp(scores - top)
    return weights / jnp.sum(weights, axis=-1, keepdims=True)


def kernel(
    q_ref, k_ref, v_ref, context_ref, residual_ref, codes_ref, scales_ref, gain_ref, weight_ref, lengths_ref,
    out_ref,
    context, residual, codes, scales, gain, weight,
    q_all, k_all, v_all, part, sums, text, squares, rows, kv_own, kv_all, attended,
    load_sem, own_sem, send_sem, recv_sem,
):
    g = lax.axis_index("grp")
    me = lax.axis_index("seq")
    mine = block_of(me)

    barrier = pltpu.get_barrier_semaphore()

    def greet(i, carry):
        pl.semaphore_signal(barrier, inc=1, device_id={"seq": partner(me, i)}, device_id_type=MESH)
        return carry

    lax.fori_loop(1, 64, greet, 0)
    for i in range(1, 8):
        pl.semaphore_signal(barrier, inc=1, device_id={"grp": (g + i) % 8}, device_id_type=MESH)

    loads = [
        pltpu.make_async_copy(src, dst, load_sem.at[n])
        for n, (src, dst) in enumerate(
            (
                (context_ref, context),
                (codes_ref, codes),
                (scales_ref, scales),
                (residual_ref, residual),
                (gain_ref, gain),
                (weight_ref, weight),
            )
        )
    ]
    for load in loads:
        load.start()
    own = [
        pltpu.make_async_copy(src.at[mine], dst.at[:, me], own_sem.at[n])
        for n, (src, dst) in enumerate(((q_ref, q_all), (k_ref, k_all), (v_ref, v_all)))
    ]
    for copy in own:
        copy.start()
    kv_own[...] = jnp.zeros_like(kv_own)
    squares[me] = jnp.zeros((2, 128), F32)

    for load in loads[:3]:
        load.wait()
    level = jnp.concatenate([jnp.broadcast_to(scales[n : n + 1, :], (128, 64)).T for n in range(4)], axis=1)
    dense = (codes[...].astype(F32) * level).astype(BF16)
    dense = jnp.concatenate([dense, dense], axis=0)
    product = dot_t(context[...], dense).reshape(8, 2, 16, 128)
    half = lax.broadcasted_iota(jnp.int32, (16, 128), 1) // 64
    first = half == me % 2
    part[...] = jnp.where(first[None], product[:, 0], product[:, 1])
    sums[g] = part[g]

    pl.semaphore_wait(barrier, 70)

    for i in (4, 5, 3, 2, 6, 1, 7):
        to = (g + i) % 8
        pltpu.make_async_remote_copy(
            part.at[to], sums.at[g], send_sem.at[0], recv_sem.at[0], device_id={"grp": to}, device_id_type=MESH
        ).start()

    def send_tokens(i, carry):
        to = partner(me, i)
        block = block_of(to)
        for n, (src, dst) in enumerate(((k_ref, k_all), (q_ref, q_all), (v_ref, v_all))):
            pltpu.make_async_remote_copy(
                src.at[block],
                dst.at[:, me],
                send_sem.at[1 + n],
                recv_sem.at[1 + n],
                device_id={"seq": to},
                device_id_type=MESH,
            ).start()
        return carry

    lax.fori_loop(1, 64, send_tokens, 0)

    loads[3].wait()
    loads[4].wait()
    start = residual[...].astype(F32)
    start = jnp.concatenate([start, start], axis=1)
    start = jnp.where(first, start[:16], start[16:])
    wide_gain = jnp.concatenate([gain[...], gain[...]], axis=1)
    wait_bytes(sums.at[0:7], recv_sem.at[0])
    hidden = start + jnp.sum(sums[...], axis=0)
    text[me] = (hidden * wide_gain).astype(BF16)
    pick = (lax.broadcasted_iota(jnp.int32, (2, 128), 0) == (lax.broadcasted_iota(jnp.int32, (2, 128), 1) // 64 + me) % 2)
    squares[me, :, 0:16] = lax.dot_general(
        pick.astype(F32),
        hidden * hidden,
        (((1,), (1,)), ((), ())),
        preferred_element_type=F32,
        precision=lax.Precision.HIGHEST,
    )

    def send_text(i, carry):
        to = partner(me, i)
        for n, buf in enumerate((text, squares)):
            pltpu.make_async_remote_copy(
                buf.at[me],
                buf.at[me],
                send_sem.at[4 + n],
                recv_sem.at[4 + n],
                device_id={"seq": to},
                device_id_type=MESH,
            ).start()
        return carry

    lax.fori_loop(1, 64, send_text, 0)

    wait_bytes(squares.at[0:63], recv_sem.at[5])
    norm = lax.rsqrt(jnp.sum(squares[...], axis=0) / D_TEXT + 1e-06)
    diagonal = lax.broadcasted_iota(jnp.int32, (16, 128), 0) == lax.broadcasted_iota(jnp.int32, (16, 128), 1)
    norm = jnp.concatenate(
        [jnp.sum(jnp.where(diagonal, norm[n : n + 1], 0.0), axis=1, keepdims=True) for n in range(2)], axis=0
    )
    wait_bytes(text.at[0:63], recv_sem.at[4])
    pairs = text[...].reshape(32, 2, 16, 128)
    even, odd = pairs[:, 0], pairs[:, 1]
    left = (half == 0)[None]
    upper = jnp.where(left, even, odd)
    lower = jnp.where(left, odd, even).astype(F32).reshape(512, 128)
    lower = pltpu.roll(lower, 64, 1).reshape(32, 16, 128).astype(BF16)
    for n in range(32):
        rows[0:16, 128 * n : 128 * n + 128] = upper[n]
        rows[16:32, 128 * n : 128 * n + 128] = lower[n]
    loads[5].wait()
    kv_own[:, 0:96] = (dot_t(rows[...], weight[...]) * norm).astype(BF16)

    prompt, triple = g // 2, (me % 32) // 4
    slot = (me // 32) * 4 + me % 4

    def send_kv(i, carry):
        z = (triple // 2 + 2 + 4 * (i % 2)) % 8
        x = (triple % 2) * 2 + prompt // 2
        pltpu.make_async_remote_copy(
            kv_own,
            kv_all.at[slot, g % 2],
            send_sem.at[6],
            recv_sem.at[6],
            device_id={"grp": (g + i // 2) % 8, "seq": z * 8 + x * 2 + prompt % 2},
            device_id_type=MESH,
        ).start()
        return carry

    lax.fori_loop(0, 16, send_kv, 0)

    for copy in own:
        copy.wait()
    for n in range(3):
        wait_bytes(q_ref.at[0:63], recv_sem.at[1 + n])
    self_out = []
    for n in range(3):
        scores = dot_t(q_all[n].reshape(256, 128), k_all[n].reshape(256, 128)) * FACTOR
        probs = softmax_rows(scores).astype(BF16)
        self_out.append(jnp.dot(probs, v_all[n].reshape(256, 128), preferred_element_type=F32).astype(BF16))

    length = lengths_ref[(mine // 8) % 4]
    live = lax.broadcasted_iota(jnp.int32, (256, 64), 1) < length
    source = lax.broadcasted_iota(jnp.int32, (128, 384), 0)
    target = lax.broadcasted_iota(jnp.int32, (128, 384), 1)
    wait_bytes(kv_all, recv_sem.at[6])
    text_keys = jnp.zeros((64, 384), F32)
    text_values = jnp.zeros((64, 384), F32)
    for n in range(4):
        place = ((source + 96 * n == target) & (source < 96)).astype(BF16)
        text_keys += jnp.dot(kv_all[n].reshape(64, 128), place, preferred_element_type=F32)
        text_values += jnp.dot(kv_all[4 + n].reshape(64, 128), place, preferred_element_type=F32)
    text_keys, text_values = text_keys.astype(BF16), text_values.astype(BF16)
    for n in range(3):
        columns = slice(128 * n, 128 * n + 128)
        scores = dot_t(q_all[n].reshape(256, 128), text_keys[:, columns]) * FACTOR
        probs = softmax_rows(jnp.where(live, scores, -1e30)).astype(BF16)
        cross = jnp.dot(probs, text_values[:, columns], preferred_element_type=F32)
        attended[n] = (self_out[n].astype(F32) + cross).astype(BF16).reshape(64, 4, 128)

    def send_out(i, carry):
        to = partner(me, i)
        pltpu.make_async_remote_copy(
            attended.at[:, to],
            out_ref.at[mine],
            send_sem.at[7],
            recv_sem.at[7],
            device_id={"seq": to},
            device_id_type=MESH,
        ).start()
        return carry

    lax.fori_loop(1, 64, send_out, 0)
    last = pltpu.make_async_copy(attended.at[:, me], out_ref.at[mine], own_sem.at[3])
    last.start()

    wait_bytes(part.at[0:7], send_sem.at[0])
    for n in range(3):
        wait_bytes(q_ref.at[0:63], send_sem.at[1 + n])
    wait_bytes(text.at[0:63], send_sem.at[4])
    wait_bytes(squares.at[0:63], send_sem.at[5])
    wait_bytes(kv_all, send_sem.at[6])
    last.wait()
    wait_bytes(q_ref.at[0:63], send_sem.at[7])
    wait_bytes(q_ref.at[0:63], recv_sem.at[7])


def local(queries, keys, values, context, residual, codes, scales, gain, kv_weight, lengths):
    blocks = (64, 3, 4, 128)
    anywhere = pl.BlockSpec(memory_space=pl.ANY)
    tokens = pltpu.VMEM((3, 64, 4, 128), BF16)
    out = pl.pallas_call(
        kernel,
        out_shape=jax.ShapeDtypeStruct(blocks, BF16),
        in_specs=[anywhere] * 9 + [pl.BlockSpec(memory_space=pltpu.SMEM)],
        out_specs=anywhere,
        scratch_shapes=[
            pltpu.VMEM((256, 512), BF16),
            pltpu.VMEM((32, 64), BF16),
            pltpu.VMEM((64, 512), jnp.int32),
            pltpu.VMEM((4, 64), F32),
            pltpu.VMEM((1, 64), F32),
            pltpu.VMEM((96, 4096), BF16),
            tokens,
            tokens,
            tokens,
            pltpu.VMEM((8, 16, 128), F32),
            pltpu.VMEM((8, 16, 128), F32),
            pltpu.VMEM((64, 16, 128), BF16),
            pltpu.VMEM((64, 2, 128), F32),
            pltpu.VMEM((32, 4096), BF16),
            pltpu.VMEM((32, 128), BF16),
            pltpu.VMEM((8, 2, 32, 128), BF16),
            tokens,
            pltpu.SemaphoreType.DMA((6,)),
            pltpu.SemaphoreType.DMA((4,)),
            pltpu.SemaphoreType.DMA((8,)),
            pltpu.SemaphoreType.DMA((8,)),
        ],
        compiler_params=pltpu.CompilerParams(
            collective_id=0, has_side_effects=True, vmem_limit_bytes=32 * 1024 * 1024
        ),
        name="block",
    )(
        queries.reshape(blocks),
        keys.reshape(blocks),
        values.reshape(blocks),
        context,
        residual,
        codes.T,
        scales,
        gain.reshape(1, 64),
        kv_weight.T,
        lengths,
    )
    return out.reshape(queries.shape)


def solution(mesh):
    placed = (
        P("grp", None, "seq", None),
        P("grp", None, "seq", None),
        P("grp", None, "seq", None),
        P(None, "grp"),
        P("grp", "seq"),
        P("grp", "seq"),
        P("grp", "seq"),
        P("seq"),
        P(None, "seq"),
        P(),
    )
    return jax.shard_map(
        local, mesh=mesh, in_specs=placed, out_specs=P("grp", None, "seq", None), check_vma=False
    )
```

time: 861 us -> 67 us (0.08)
  the two profiles are of different devices: /device:TPU:2 before, /device:TPU:1 now
where the time goes in v1:
time: 67 us; the launch traced here: 66.7 us
  Pallas kernels  59.5 us (89%)
  local copies, waits for them, and re-layouts  7.13 us (11%)
    pallas_call x1, Pallas kernels, local(): pl.pallas_call(kernel, out_shape=jax.ShapeDtypeStruct(blocks, BF16), in_s...  59.5 us
    unnamed x21, local copies, waits for them, and re-layouts  7.13 us

profile of v1, /device:TPU:1, one launch (start us, length us, event | category | flops | bytes accessed | tf_op | source)
XLA Modules:
  0.0 66.7 jit_solution(5143438862311386093)
XLA Ops:
  0.0 0.0 copy-start.6
  0.0 0.0 copy-start.7
  0.0 0.0 copy-start.8
  0.0 0.0 copy-start.9
  0.0 0.7 %copy-done.6 = bf16[32,64]{1,0:T(8,128)(2,1)S(1)} copy-done((bf16[32,64]{1,0:T(8,128)(2,1)S(1)}, bf16[32,64]{1,0:T(8,128)(2,1)}, u32[]{:S(2)}) %copy-start.6) | copy-done | bytes 4120
  0.7 0.0 copy-done.7
  0.7 0.0 copy-done.8
  0.7 0.0 copy-done.9
  0.7 0.0 copy-start
  0.7 1.1 %copy-done = bf16[4096,96]{0,1:T(8,128)(2,1)S(1)} copy-done((bf16[4096,96]{0,1:T(8,128)(2,1)S(1)}, bf16[4096,96]{0,1:T(8,128)(2,1)}, u32[]{:S(2)}) %copy-start) | copy-done | bytes 786456
  1.8 0.0 copy-start.1
  1.8 0.9 %copy-done.1 = bf16[256,512]{1,0:T(8,128)(2,1)S(1)} copy-done((bf16[256,512]{1,0:T(8,128)(2,1)S(1)}, bf16[256,512]{1,0:T(8,128)(2,1)}, u32[]{:S(2)}) %copy-start.1) | copy-done | bytes 262168
  2.8 0.0 copy-start.2
  2.8 0.9 %copy-done.2 = bf16[8,24,4,128]{3,2,1,0:T(4,128)(2,1)S(1)} copy-done((bf16[8,24,4,128]{3,2,1,0:T(4,128)(2,1)S(1)}, bf16[8,24,4,128]{3,2,1,0:T(4,128)(2,1)}, u32[]{:S(2)}) %copy-start.2) | copy-done | bytes 196632
  3.7 0.0 copy-start.3
  3.7 0.9 %copy-done.3 = bf16[8,24,4,128]{3,2,1,0:T(4,128)(2,1)S(1)} copy-done((bf16[8,24,4,128]{3,2,1,0:T(4,128)(2,1)S(1)}, bf16[8,24,4,128]{3,2,1,0:T(4,128)(2,1)}, u32[]{:S(2)}) %copy-start.3) | copy-done | bytes 196632
  4.6 0.0 copy-start.4
  4.6 0.9 %copy-done.4 = bf16[8,24,4,128]{3,2,1,0:T(4,128)(2,1)S(1)} copy-done((bf16[8,24,4,128]{3,2,1,0:T(4,128)(2,1)S(1)}, bf16[8,24,4,128]{3,2,1,0:T(4,128)(2,1)}, u32[]{:S(2)}) %copy-start.4) | copy-done | bytes 196632
  5.6 0.0 copy-start.5
  5.6 0.9 %copy-done.5 = s32[512,64]{0,1:T(8,128)S(1)} copy-done((s32[512,64]{0,1:T(8,128)S(1)}, s32[512,64]{0,1:T(8,128)}, u32[]{:S(2)}) %copy-start.5) | copy-done | bytes 131096
  6.5 59.5 %block.1 = bf16[64,3,4,128]{3,2,1,0:T(4,128)(2,1)S(1)} custom-call(bf16[64,3,4,128]{3,2,1,0:T(4,128)(2,1)S(1)} %bitcast.9, bf16[64,3,4,128]{3,2,1,0:T(4,128)(2,1)S(1)} %bitcast.10, bf16[64,3,4,128]{3,2,1,0:T(4,128)(2,1)S(1)} %bitcast.11, bf16[256,512]{1,0:T(8,128)(2,1)S(1)} %copy-done.1, bf16[32,64]{1,0:T(8,128)(2,1)S(1)} %copy-done.6, ...), custom_call_target="tpu_custom_call" | custom-call | tf_op jit(solution)/shard_map/block/pallas_call | solution.py:253
  66.0 0.7 %copy.12 = bf16[8,24,4,128]{3,2,1,0:T(4,128)(2,1)} copy(bf16[8,24,4,128]{3,2,1,0:T(4,128)(2,1)S(1)} %bitcast.7) | data formatting | bytes 393216
Async XLA Ops:
  0.0 0.7 %copy-start.6 = (bf16[32,64]{1,0:T(8,128)(2,1)S(1)}, bf16[32,64]{1,0:T(8,128)(2,1)}, u32[]{:S(2)}) copy-start(bf16[32,64]{1,0:T(8,128)(2,1)} %residual_ref.1) | copy-start | bytes 12292
  0.0 0.7 %copy-start.7 = (f32[4,64]{1,0:T(4,128)S(1)}, f32[4,64]{1,0:T(4,128)}, u32[]{:S(2)}) copy-start(f32[4,64]{1,0:T(4,128)} %scales_ref.1) | copy-start | bytes 3076
  0.0 0.7 %copy-start.8 = (f32[64]{0:T(128)S(1)}, f32[64]{0:T(128)}, u32[]{:S(2)}) copy-start(f32[64]{0:T(128)} %param.17) | copy-start | bytes 772
  0.0 0.7 %copy-start.9 = (s32[4]{0:T(128)S(1)}, s32[4]{0:T(128)}, u32[]{:S(2)}) copy-start(s32[4]{0:T(128)} %lengths_ref.1) | copy-start | bytes 52
  0.7 1.1 %copy-start = (bf16[4096,96]{0,1:T(8,128)(2,1)S(1)}, bf16[4096,96]{0,1:T(8,128)(2,1)}, u32[]{:S(2)}) copy-start(bf16[4096,96]{0,1:T(8,128)(2,1)} %param.18) | copy-start | bytes 2359300
  1.8 0.9 %copy-start.1 = (bf16[256,512]{1,0:T(8,128)(2,1)S(1)}, bf16[256,512]{1,0:T(8,128)(2,1)}, u32[]{:S(2)}) copy-start(bf16[256,512]{1,0:T(8,128)(2,1)} %context_ref.1) | copy-start | bytes 786436
  2.8 0.9 %copy-start.2 = (bf16[8,24,4,128]{3,2,1,0:T(4,128)(2,1)S(1)}, bf16[8,24,4,128]{3,2,1,0:T(4,128)(2,1)}, u32[]{:S(2)}) copy-start(bf16[8,24,4,128]{3,2,1,0:T(4,128)(2,1)} %param.10) | copy-start | bytes 589828
  3.7 0.9 %copy-start.3 = (bf16[8,24,4,128]{3,2,1,0:T(4,128)(2,1)S(1)}, bf16[8,24,4,128]{3,2,1,0:T(4,128)(2,1)}, u32[]{:S(2)}) copy-start(bf16[8,24,4,128]{3,2,1,0:T(4,128)(2,1)} %param.11) | copy-start | bytes 589828
  4.6 0.9 %copy-start.4 = (bf16[8,24,4,128]{3,2,1,0:T(4,128)(2,1)S(1)}, bf16[8,24,4,128]{3,2,1,0:T(4,128)(2,1)}, u32[]{:S(2)}) copy-start(bf16[8,24,4,128]{3,2,1,0:T(4,128)(2,1)} %param.12) | copy-start | bytes 589828
  5.6 0.9 %copy-start.5 = (s32[512,64]{0,1:T(8,128)S(1)}, s32[512,64]{0,1:T(8,128)}, u32[]{:S(2)}) copy-start(s32[512,64]{0,1:T(8,128)} %param.15) | copy-start | bytes 393220

commit v2 on v1

v2 whole, which is shorter than its diff:
```python
import math

import jax
import jax.numpy as jnp
from jax import lax
from jax.experimental import pallas as pl
from jax.experimental.pallas import tpu as pltpu
from jax.sharding import PartitionSpec as P

MESH = pl.DeviceIdType.MESH
BF16 = jnp.bfloat16
F32 = jnp.float32
FACTOR = 1.0 / math.sqrt(128)
D_TEXT = 4096


def dot_t(a, b):
    return lax.dot_general(a, b, (((1,), (1,)), ((), ())), preferred_element_type=F32)


def partner(me, dz, dxy):
    z, x, y = me // 8, (me // 2) % 4, me % 2
    return ((z + dz) % 8) * 8 + ((x + dxy // 2) % 4) * 2 + (y + dxy) % 2


def block_of(p):
    z, x, y = p // 8, (p // 2) % 4, p % 2
    t = (z + 6) % 8
    return ((t // 4) * 4 + (x % 2) * 2 + y) * 8 + (t % 4) * 2 + x // 2


def wait_bytes(ref, sem):
    pltpu.make_async_copy(ref, ref, sem).wait()


def softmax_rows(scores):
    top = jnp.max(scores, axis=-1, keepdims=True)
    weights = jnp.exp(scores - top)
    return weights / jnp.sum(weights, axis=-1, keepdims=True)


def kernel(
    q_ref, k_ref, v_ref, context_ref, residual_ref, codes_ref, scales_ref, gain_ref, weight_ref, lengths_ref,
    out_ref,
    context, residual, codes, scales, gain, weight,
    q_all, k_all, v_all, part, sums, text, squares_z, squares, rows, kv_own, kv_all, attended,
    load_sem, own_sem, send_sem, recv_sem, ready_sem,
):
    g = lax.axis_index("grp")
    me = lax.axis_index("seq")
    z, xy = me // 8, me % 8
    mine = block_of(me)

    barrier = pltpu.get_barrier_semaphore()
    for i in (4, 5, 3, 2, 6, 1, 7):
        pl.semaphore_signal(barrier, inc=1, device_id={"grp": (g + i) % 8}, device_id_type=MESH)
        pl.semaphore_signal(barrier, inc=1, device_id={"seq": partner(me, i, 0)}, device_id_type=MESH)
        pl.semaphore_signal(barrier, inc=1, device_id={"seq": partner(me, 0, i)}, device_id_type=MESH)

    loads = [
        pltpu.make_async_copy(src, dst, load_sem.at[n])
        for n, (src, dst) in enumerate(
            (
                (codes_ref, codes),
                (scales_ref, scales),
                (context_ref, context),
                (residual_ref, residual),
                (gain_ref, gain),
                (weight_ref, weight),
            )
        )
    ]
    for load in loads:
        load.start()
    arrays = ((k_ref, k_all), (q_ref, q_all), (v_ref, v_all))
    own = [pltpu.make_async_copy(src.at[mine], dst.at[:, me], own_sem.at[n]) for n, (src, dst) in enumerate(arrays)]
    for copy in own:
        copy.start()
    kv_own[...] = jnp.zeros_like(kv_own)
    squares_z[z] = jnp.zeros((2, 128), F32)

    for load in loads[:3]:
        load.wait()
    level = jnp.concatenate([jnp.broadcast_to(scales[n : n + 1, :], (128, 64)).T for n in range(4)], axis=1)
    dense = (codes[...].astype(F32) * level).astype(BF16)
    dense = jnp.concatenate([dense, dense], axis=0)
    product = dot_t(context[...], dense).reshape(8, 2, 16, 128)
    half = lax.broadcasted_iota(jnp.int32, (16, 128), 1) // 64
    first = half == me % 2
    part[...] = jnp.where(first[None], product[:, 0], product[:, 1])
    sums[g] = part[g]

    pl.semaphore_wait(barrier, 21)

    for i in (4, 5, 3, 2, 6, 1, 7):
        to = (g + i) % 8
        pltpu.make_async_remote_copy(
            part.at[to], sums.at[g], send_sem.at[0], recv_sem.at[0], device_id={"grp": to}, device_id_type=MESH
        ).start()
    for i in (4, 3, 5, 2, 6, 1, 7):
        pl.semaphore_signal(ready_sem, inc=1, device_id={"seq": partner(me, i, 0)}, device_id_type=MESH)

    def send_tokens(n, to):
        src, dst = arrays[n]
        pltpu.make_async_remote_copy(
            src.at[block_of(to)],
            dst.at[:, me],
            send_sem.at[1 + n],
            recv_sem.at[1 + n],
            device_id={"seq": to},
            device_id_type=MESH,
        ).start()

    def send_near(n):
        for i in (4, 3, 5, 2, 6, 1, 7):
            send_tokens(n, partner(me, i, 0))
            send_tokens(n, partner(me, 0, i))

    def send_far(n):
        def step(i, carry):
            send_tokens(n, partner(me, 1 + (i * 3) % 7, 1 + i // 7))
            return carry

        lax.fori_loop(0, 49, step, 0)

    for n in (0, 1, 2):
        send_near(n)

    loads[3].wait()
    loads[4].wait()
    start = residual[...].astype(F32)
    start = jnp.concatenate([start, start], axis=1)
    start = jnp.where(first, start[:16], start[16:])
    wide_gain = jnp.concatenate([gain[...], gain[...]], axis=1)
    pl.semaphore_wait(ready_sem, 7)
    for n in (0,):
        send_far(n)
    wait_bytes(sums.at[0:7], recv_sem.at[0])
    hidden = start + jnp.sum(sums[...], axis=0)
    text[xy, z] = (hidden * wide_gain).astype(BF16)
    pick = lax.broadcasted_iota(jnp.int32, (2, 128), 0) == (lax.broadcasted_iota(jnp.int32, (2, 128), 1) // 64 + me) % 2
    squares_z[z, :, 0:16] = lax.dot_general(
        pick.astype(F32),
        hidden * hidden,
        (((1,), (1,)), ((), ())),
        preferred_element_type=F32,
        precision=lax.Precision.HIGHEST,
    )

    def send_line(buf, at, n, to):
        pltpu.make_async_remote_copy(
            buf.at[at], buf.at[at], send_sem.at[n], recv_sem.at[n], device_id={"seq": to}, device_id_type=MESH
        ).start()

    for i in (4, 3, 5, 2, 6, 1, 7):
        send_line(text, (xy, z), 10 + z, partner(me, i, 0))

    def forward(plane):
        @pl.when(plane != z)
        def _():
            wait_bytes(text.at[0, 0], recv_sem.at[10 + plane])

        for i in (5, 4, 7, 6, 3, 2, 1):
            send_line(text, (xy, plane), 6, partner(me, 0, i))

    for i in (4, 3, 5, 2, 6, 1, 7):
        send_line(squares_z, z, 5, partner(me, i, 0))
    for n in (1,):
        send_far(n)

    def forward_one(i, carry):
        forward(i)
        return carry

    lax.fori_loop(0, 8, forward_one, 0)
    wait_bytes(squares_z.at[0:7], recv_sem.at[5])
    squares[xy] = jnp.sum(squares_z[...], axis=0)
    for i in (5, 4, 7, 6, 3, 2, 1):
        send_line(squares, xy, 7, partner(me, 0, i))
    for n in (2,):
        send_far(n)

    wait_bytes(squares.at[0:7], recv_sem.at[7])
    norm = lax.rsqrt(jnp.sum(squares[...], axis=0) / D_TEXT + 1e-06)
    diagonal = lax.broadcasted_iota(jnp.int32, (16, 128), 0) == lax.broadcasted_iota(jnp.int32, (16, 128), 1)
    norm = jnp.concatenate(
        [jnp.sum(jnp.where(diagonal, norm[n : n + 1], 0.0), axis=1, keepdims=True) for n in range(2)], axis=0
    )
    wait_bytes(text.at[0:7], recv_sem.at[6])
    left = (half == 0)[None]
    for x in range(4):
        even, odd = text[2 * x], text[2 * x + 1]
        upper = jnp.where(left, even, odd)
        lower = jnp.where(left, odd, even).astype(F32).reshape(128, 128)
        lower = pltpu.roll(lower, 64, 1).reshape(8, 16, 128).astype(BF16)
        for n in range(8):
            at = 128 * (4 * n + x)
            rows[0:16, at : at + 128] = upper[n]
            rows[16:32, at : at + 128] = lower[n]
    loads[5].wait()
    kv_own[:, 0:96] = (dot_t(rows[...], weight[...]) * norm).astype(BF16)

    prompt, triple = g // 2, (me % 32) // 4
    slot = (me // 32) * 4 + me % 4

    def send_kv(i, carry):
        to_z = (triple // 2 + 2 + 4 * (i % 2)) % 8
        to_x = (triple % 2) * 2 + prompt // 2
        pltpu.make_async_remote_copy(
            kv_own,
            kv_all.at[slot, g % 2],
            send_sem.at[8],
            recv_sem.at[8],
            device_id={"grp": (g + 4 + i // 2) % 8, "seq": to_z * 8 + to_x * 2 + prompt % 2},
            device_id_type=MESH,
        ).start()
        return carry

    lax.fori_loop(0, 16, send_kv, 0)
    for n in ():
        send_far(n)

    for copy in own:
        copy.wait()
    for n in range(3):
        wait_bytes(q_ref.at[0:63], recv_sem.at[1 + n])
    self_out = []
    for n in range(3):
        scores = dot_t(q_all[n].reshape(256, 128), k_all[n].reshape(256, 128)) * FACTOR
        probs = softmax_rows(scores).astype(BF16)
        self_out.append(jnp.dot(probs, v_all[n].reshape(256, 128), preferred_element_type=F32).astype(BF16))

    length = lengths_ref[(mine // 8) % 4]
    live = lax.broadcasted_iota(jnp.int32, (256, 64), 1) < length
    source = lax.broadcasted_iota(jnp.int32, (128, 384), 0)
    target = lax.broadcasted_iota(jnp.int32, (128, 384), 1)
    places = [((source + 96 * n == target) & (source < 96)).astype(BF16) for n in range(4)]
    wait_bytes(kv_all, recv_sem.at[8])
    text_keys = jnp.zeros((64, 384), F32)
    text_values = jnp.zeros((64, 384), F32)
    for n in range(4):
        text_keys += jnp.dot(kv_all[n].reshape(64, 128), places[n], preferred_element_type=F32)
        text_values += jnp.dot(kv_all[4 + n].reshape(64, 128), places[n], preferred_element_type=F32)
    text_keys, text_values = text_keys.astype(BF16), text_values.astype(BF16)
    for n in range(3):
        columns = slice(128 * n, 128 * n + 128)
        scores = dot_t(q_all[n].reshape(256, 128), text_keys[:, columns]) * FACTOR
        probs = softmax_rows(jnp.where(live, scores, -1e30)).astype(BF16)
        cross = jnp.dot(probs, text_values[:, columns], preferred_element_type=F32)
        attended[n] = (self_out[n].astype(F32) + cross).astype(BF16).reshape(64, 4, 128)

    def send_out(i, carry):
        to_z = i // 8
        to = to_z * 8 + ((xy // 2 + (i % 8) // 2) % 4) * 2 + (xy + i) % 2
        pltpu.make_async_remote_copy(
            attended.at[:, to],
            out_ref.at[mine],
            send_sem.at[9],
            recv_sem.at[9],
            device_id={"seq": to},
            device_id_type=MESH,
        ).start()
        return carry

    lax.fori_loop(0, z * 8, send_out, 0)
    lax.fori_loop(z * 8 + 1, 64, send_out, 0)
    last = pltpu.make_async_copy(attended.at[:, me], out_ref.at[mine], own_sem.at[3])
    last.start()

    wait_bytes(part.at[0:7], send_sem.at[0])
    for n in range(3):
        wait_bytes(q_ref.at[0:63], send_sem.at[1 + n])
    wait_bytes(text.at[0, 0:7], send_sem.at[10 + z])
    wait_bytes(squares_z.at[0:7], send_sem.at[5])
    wait_bytes(text.at[0:7], send_sem.at[6])
    wait_bytes(squares.at[0:7], send_sem.at[7])
    wait_bytes(kv_all, send_sem.at[8])
    last.wait()
    wait_bytes(q_ref.at[0:63], send_sem.at[9])
    wait_bytes(q_ref.at[0:63], recv_sem.at[9])


def local(queries, keys, values, context, residual, codes, scales, gain, kv_weight, lengths):
    blocks = (64, 3, 4, 128)
    anywhere = pl.BlockSpec(memory_space=pl.ANY)
    tokens = pltpu.VMEM((3, 64, 4, 128), BF16)
    out = pl.pallas_call(
        kernel,
        out_shape=pltpu.VMEM(blocks, BF16),
        in_specs=[anywhere] * 9 + [pl.BlockSpec(memory_space=pltpu.SMEM)],
        out_specs=pl.BlockSpec(memory_space=pltpu.VMEM),
        scratch_shapes=[
            pltpu.VMEM((256, 512), BF16),
            pltpu.VMEM((32, 64), BF16),
            pltpu.VMEM((64, 512), jnp.int32),
            pltpu.VMEM((4, 64), F32),
            pltpu.VMEM((1, 64), F32),
            pltpu.VMEM((96, 4096), BF16),
            tokens,
            tokens,
            tokens,
            pltpu.VMEM((8, 16, 128), F32),
            pltpu.VMEM((8, 16, 128), F32),
            pltpu.VMEM((8, 8, 16, 128), BF16),
            pltpu.VMEM((8, 2, 128), F32),
            pltpu.VMEM((8, 2, 128), F32),
            pltpu.VMEM((32, 4096), BF16),
            pltpu.VMEM((32, 128), BF16),
            pltpu.VMEM((8, 2, 32, 128), BF16),
            tokens,
            pltpu.SemaphoreType.DMA((6,)),
            pltpu.SemaphoreType.DMA((4,)),
            pltpu.SemaphoreType.DMA((18,)),
            pltpu.SemaphoreType.DMA((18,)),
            pltpu.SemaphoreType.REGULAR,
        ],
        compiler_params=pltpu.CompilerParams(
            collective_id=0, has_side_effects=True, vmem_limit_bytes=60 * 1024 * 1024
        ),
        name="block",
    )(
        queries.reshape(blocks),
        keys.reshape(blocks),
        values.reshape(blocks),
        context,
        residual,
        codes.T,
        scales,
        gain.reshape(1, 64),
        kv_weight.T,
        lengths,
    )
    return out.reshape(queries.shape)


def solution(mesh):
    placed = (
        P("grp", None, "seq", None),
        P("grp", None, "seq", None),
        P("grp", None, "seq", None),
        P(None, "grp"),
        P("grp", "seq"),
        P("grp", "seq"),
        P("grp", "seq"),
        P("seq"),
        P(None, "seq"),
        P(),
    )
    return jax.shard_map(
        local, mesh=mesh, in_specs=placed, out_specs=P("grp", None, "seq", None), check_vma=False
    )
```

time: 67 us -> 49.4 us (0.74)
  Pallas kernels: 59.5 us -> 48.5 us
  local copies, waits for them, and re-layouts: 7.13 us -> 0.68 us
    pallas_call x1, Pallas kernels: 59.5 us -> 48.5 us  [local(): pl.pallas_call(kernel, out_shape=pltpu.VMEM(blocks, BF16), in_specs=[anyw...]
    unnamed x21 -> x1, local copies, waits for them, and re-layouts: 7.13 us -> 0.68 us
where the time goes in v2:
time: 49.4 us; the launch traced here: 49.2 us
  Pallas kernels  48.5 us (98%)
  local copies, waits for them, and re-layouts  0.68 us (1%)
    pallas_call x1, Pallas kernels, local(): pl.pallas_call(kernel, out_shape=pltpu.VMEM(blocks, BF16), in_specs=[anyw...  48.5 us

profile of v2, /device:TPU:1, one launch (start us, length us, event | category | flops | bytes accessed | tf_op | source)
XLA Modules:
  0.0 49.2 jit_solution(3325555778920412440)
XLA Ops:
  0.0 48.5 %block.1 = bf16[64,3,4,128]{3,2,1,0:T(4,128)(2,1)S(1)} custom-call(bf16[64,3,4,128]{3,2,1,0:T(4,128)(2,1)} %bitcast.9, bf16[64,3,4,128]{3,2,1,0:T(4,128)(2,1)} %bitcast.10, bf16[64,3,4,128]{3,2,1,0:T(4,128)(2,1)} %bitcast.11, bf16[256,512]{1,0:T(8,128)(2,1)} %context_ref.1, bf16[32,64]{1,0:T(8,128)(2,1)} %residual_ref.1, s32[64,512]{1,0:T(8,128)} %bitcast.12, ...), custom_call_target="tpu_custom_call" | custom-call | tf_op jit(solution)/shard_map/block/pallas_call | solution.py:287
  48.5 0.7 %copy.12 = bf16[8,24,4,128]{3,2,1,0:T(4,128)(2,1)} copy(bf16[8,24,4,128]{3,2,1,0:T(4,128)(2,1)S(1)} %bitcast.7) | data formatting | bytes 393216

commit v3 on v2

--- a/solution.py
+++ b/solution.py
@@ -116,14 +116,14 @@
             send_tokens(n, partner(me, i, 0))
             send_tokens(n, partner(me, 0, i))
 
-    def send_far(n):
+    def send_part(n, low, high):
         def step(i, carry):
             send_tokens(n, partner(me, 1 + (i * 3) % 7, 1 + i // 7))
             return carry
 
-        lax.fori_loop(0, 49, step, 0)
-
-    for n in (0, 1, 2):
+        lax.fori_loop(low, high, step, 0)
+
+    for n in range(3):
         send_near(n)
 
     loads[3].wait()
@@ -133,8 +133,7 @@
     start = jnp.where(first, start[:16], start[16:])
     wide_gain = jnp.concatenate([gain[...], gain[...]], axis=1)
     pl.semaphore_wait(ready_sem, 7)
-    for n in (0,):
-        send_far(n)
+    send_part(0, 0, 28)
     wait_bytes(sums.at[0:7], recv_sem.at[0])
     hidden = start + jnp.sum(sums[...], axis=0)
     text[xy, z] = (hidden * wide_gain).astype(BF16)
@@ -165,8 +164,9 @@
 
     for i in (4, 3, 5, 2, 6, 1, 7):
         send_line(squares_z, z, 5, partner(me, i, 0))
-    for n in (1,):
-        send_far(n)
+
+    send_part(0, 28, 49)
+    send_part(1, 0, 35)
 
     def forward_one(i, carry):
         forward(i)
@@ -177,8 +177,8 @@
     squares[xy] = jnp.sum(squares_z[...], axis=0)
     for i in (5, 4, 7, 6, 3, 2, 1):
         send_line(squares, xy, 7, partner(me, 0, i))
-    for n in (2,):
-        send_far(n)
+    send_part(1, 35, 49)
+    send_part(2, 0, 49)
 
     wait_bytes(squares.at[0:7], recv_sem.at[7])
     norm = lax.rsqrt(jnp.sum(squares[...], axis=0) / D_TEXT + 1e-06)
@@ -211,14 +211,12 @@
             kv_all.at[slot, g % 2],
             send_sem.at[8],
             recv_sem.at[8],
-            device_id={"grp": (g + 4 + i // 2) % 8, "seq": to_z * 8 + to_x * 2 + prompt % 2},
+            device_id={"grp": i // 2, "seq": to_z * 8 + to_x * 2 + prompt % 2},
             device_id_type=MESH,
         ).start()
         return carry
 
     lax.fori_loop(0, 16, send_kv, 0)
-    for n in ():
-        send_far(n)
 
     for copy in own:
         copy.wait()

time: 49.4 us -> 47.5 us (0.962)
  Pallas kernels: 48.5 us -> 46.6 us
    pallas_call x1, Pallas kernels: 48.5 us -> 46.6 us  [local(): pl.pallas_call(kernel, out_shape=pltpu.VMEM(blocks, BF16), in_specs=[anyw...]
where the time goes in v3:
time: 47.5 us; the launch traced here: 47.3 us
  Pallas kernels  46.6 us (98%)
  local copies, waits for them, and re-layouts  0.68 us (1%)
    pallas_call x1, Pallas kernels, local(): pl.pallas_call(kernel, out_shape=pltpu.VMEM(blocks, BF16), in_specs=[anyw...  46.6 us

profile of v3, /device:TPU:1, one launch (start us, length us, event | category | flops | bytes accessed | tf_op | source)
XLA Modules:
  0.0 47.3 jit_solution(13020906547951285427)
XLA Ops:
  0.0 46.6 %block.1 = bf16[64,3,4,128]{3,2,1,0:T(4,128)(2,1)S(1)} custom-call(bf16[64,3,4,128]{3,2,1,0:T(4,128)(2,1)} %bitcast.9, bf16[64,3,4,128]{3,2,1,0:T(4,128)(2,1)} %bitcast.10, bf16[64,3,4,128]{3,2,1,0:T(4,128)(2,1)} %bitcast.11, bf16[256,512]{1,0:T(8,128)(2,1)} %context_ref.1, bf16[32,64]{1,0:T(8,128)(2,1)} %residual_ref.1, s32[64,512]{1,0:T(8,128)} %bitcast.12, ...), custom_call_target="tpu_custom_call" | custom-call | tf_op jit(solution)/shard_map/block/pallas_call | solution.py:285
  46.6 0.7 %copy.12 = bf16[8,24,4,128]{3,2,1,0:T(4,128)(2,1)} copy(bf16[8,24,4,128]{3,2,1,0:T(4,128)(2,1)S(1)} %bitcast.7) | data formatting | bytes 393216

commit v4 on v3

--- a/solution.py
+++ b/solution.py
@@ -155,21 +155,22 @@
         send_line(text, (xy, z), 10 + z, partner(me, i, 0))
 
     def forward(plane):
-        @pl.when(plane != z)
-        def _():
-            wait_bytes(text.at[0, 0], recv_sem.at[10 + plane])
-
         for i in (5, 4, 7, 6, 3, 2, 1):
             send_line(text, (xy, plane), 6, partner(me, 0, i))
 
     for i in (4, 3, 5, 2, 6, 1, 7):
         send_line(squares_z, z, 5, partner(me, i, 0))
 
+    forward(z)
     send_part(0, 28, 49)
     send_part(1, 0, 35)
 
     def forward_one(i, carry):
-        forward(i)
+        @pl.when(i != z)
+        def _():
+            wait_bytes(text.at[0, 0], recv_sem.at[10 + i])
+            forward(i)
+
         return carry
 
     lax.fori_loop(0, 8, forward_one, 0)

time: 47.5 us -> 47.1 us (level)
  no operation moved by 1% of the time
where the time goes in v4:
time: 47.1 us; the launch traced here: 47 us
  Pallas kernels  46.3 us (98%)
  local copies, waits for them, and re-layouts  0.68 us (1%)
    pallas_call x1, Pallas kernels, local(): pl.pallas_call(kernel, out_shape=pltpu.VMEM(blocks, BF16), in_specs=[anyw...  46.3 us

profile of v4, /device:TPU:1, one launch (start us, length us, event | category | flops | bytes accessed | tf_op | source)
XLA Modules:
  0.0 47.0 jit_solution(9934421345662895189)
XLA Ops:
  0.0 46.3 %block.1 = bf16[64,3,4,128]{3,2,1,0:T(4,128)(2,1)S(1)} custom-call(bf16[64,3,4,128]{3,2,1,0:T(4,128)(2,1)} %bitcast.9, bf16[64,3,4,128]{3,2,1,0:T(4,128)(2,1)} %bitcast.10, bf16[64,3,4,128]{3,2,1,0:T(4,128)(2,1)} %bitcast.11, bf16[256,512]{1,0:T(8,128)(2,1)} %context_ref.1, bf16[32,64]{1,0:T(8,128)(2,1)} %residual_ref.1, s32[64,512]{1,0:T(8,128)} %bitcast.12, ...), custom_call_target="tpu_custom_call" | custom-call | tf_op jit(solution)/shard_map/block/pallas_call | solution.py:286
  46.3 0.7 %copy.12 = bf16[8,24,4,128]{3,2,1,0:T(4,128)(2,1)} copy(bf16[8,24,4,128]{3,2,1,0:T(4,128)(2,1)S(1)} %bitcast.7) | data formatting | bytes 393216

commit v5 on v4

--- a/solution.py
+++ b/solution.py
@@ -250,7 +250,7 @@
 
     def send_out(i, carry):
         to_z = i // 8
-        to = to_z * 8 + ((xy // 2 + (i % 8) // 2) % 4) * 2 + (xy + i) % 2
+        to = to_z * 8 + i % 8
         pltpu.make_async_remote_copy(
             attended.at[:, to],
             out_ref.at[mine],
@@ -261,8 +261,8 @@
         ).start()
         return carry
 
-    lax.fori_loop(0, z * 8, send_out, 0)
-    lax.fori_loop(z * 8 + 1, 64, send_out, 0)
+    lax.fori_loop(0, me, send_out, 0)
+    lax.fori_loop(me + 1, 64, send_out, 0)
     last = pltpu.make_async_copy(attended.at[:, me], out_ref.at[mine], own_sem.at[3])
     last.start()
 

time: 47.1 us -> 47.2 us (level)
  no operation moved by 1% of the time
where the time goes in v5:
time: 47.2 us; the launch traced here: 47 us
  Pallas kernels  46.4 us (98%)
  local copies, waits for them, and re-layouts  0.68 us (1%)
    pallas_call x1, Pallas kernels, local(): pl.pallas_call(kernel, out_shape=pltpu.VMEM(blocks, BF16), in_specs=[anyw...  46.4 us

profile of v5, /device:TPU:1, one launch (start us, length us, event | category | flops | bytes accessed | tf_op | source)
XLA Modules:
  0.0 47.0 jit_solution(2947972782752300388)
XLA Ops:
  0.0 46.4 %block.1 = bf16[64,3,4,128]{3,2,1,0:T(4,128)(2,1)S(1)} custom-call(bf16[64,3,4,128]{3,2,1,0:T(4,128)(2,1)} %bitcast.9, bf16[64,3,4,128]{3,2,1,0:T(4,128)(2,1)} %bitcast.10, bf16[64,3,4,128]{3,2,1,0:T(4,128)(2,1)} %bitcast.11, bf16[256,512]{1,0:T(8,128)(2,1)} %context_ref.1, bf16[32,64]{1,0:T(8,128)(2,1)} %residual_ref.1, s32[64,512]{1,0:T(8,128)} %bitcast.12, ...), custom_call_target="tpu_custom_call" | custom-call | tf_op jit(solution)/shard_map/block/pallas_call | solution.py:286
  46.4 0.7 %copy.12 = bf16[8,24,4,128]{3,2,1,0:T(4,128)(2,1)} copy(bf16[8,24,4,128]{3,2,1,0:T(4,128)(2,1)S(1)} %bitcast.7) | data formatting | bytes 393216
